TPU v7x, 512 devices: a whole 4x8x8 slice. The times are simulated.
512 devices in a mesh: ta: 8 (over z), ha: 8 (over y), wa: 8 (over x, core).
Axes of the slice: x: 4, y: 8, z: 8, core: 2. Of those that a mesh axis runs over, the one named last changes fastest.
Arguments:
- features: float32 [16, 64, 128, 256], P('ta', 'ha', 'wa'), may hold values from -40 to 40
- cotangent: float32 [16, 64, 128, 256], P('ta', 'ha', 'wa'), may hold values from -6 to 6
- conv_one: bfloat16 [3, 2304, 256], P(None, ('ha', 'wa')), may hold values from -0.078125 to 0.078125
- conv_two: bfloat16 [3, 2304, 256], P(None, ('ha', 'wa')), may hold values from -0.078125 to 0.078125
- gain_one: float32 [256], replicated, may hold values from 0.25 to 1.75
- bias_one: float32 [256], replicated, may hold values from -3 to 3
- gain_two: float32 [256], replicated, may hold values from 0.25 to 1.75
- bias_two: float32 [256], replicated, may hold values from -3 to 3
Outputs:
- block_out: float32 [16, 64, 128, 256], P('ta', 'ha', 'wa')
- grad_input: float32 [16, 64, 128, 256], P('ta', 'ha', 'wa')
- norm_grads: float32 [4, 256], replicated
All inputs are finite; a program needn't handle non-finite values.
Results may differ from a plain program's by a relative error of at most 0.0041.
Values may be sent and summed in bfloat16 or wider, within the bound.
A program may use at most 64 MiB of HBM per device.

v0:
```python
import jax
import jax.numpy as jnp
from jax import lax
from jax.sharding import PartitionSpec as P

GROUPS = 32


epsilon = 1e-06


def from_behind(value, axis, steps):
    count = lax.axis_size(axis)
    leading, last = (max(0, -steps), min(count, count - steps))
    return lax.ppermute(value, axis, [(source, source + steps) for source in range(leading, last)])


def extended(block, sides, width):
    for axis, dim in sides:
        count = lax.axis_size(axis)
        forward = [(i, i + 1) for i in range(count - 1)]
        backward = [(target, source) for source, target in forward]
        low = lax.ppermute(
            lax.slice_in_dim(block, block.shape[dim] - width, None, axis=dim), axis, forward
        )
        high = lax.ppermute(lax.slice_in_dim(block, 0, width, axis=dim), axis, backward)
        block = jnp.concatenate([low, block, high], axis=dim)
    return block


def clip_members(field, groups):
    devices = lax.axis_size("ta") * lax.axis_size("ha") * lax.axis_size("wa")
    return field.shape[0] * field.shape[1] * field.shape[2] * devices * (field.shape[3] // groups)


def normalize(field, gain, bias, groups):
    chans = field.shape[3]
    members = clip_members(field, groups)
    totals = lax.psum(jnp.sum(field, axis=(0, 1, 2)), ("ta", "ha", "wa"))
    centre = jnp.repeat(totals.reshape(groups, -1).sum(1) / members, chans // groups)
    deviation = field - centre
    squares = lax.psum(jnp.sum(deviation * deviation, axis=(0, 1, 2)), ("ta", "ha", "wa"))
    spread = jnp.repeat(squares.reshape(groups, -1).sum(1) / members, chans // groups)
    inv_std = 1.0 / jnp.sqrt(spread + epsilon)
    unit = deviation * inv_std
    inner = unit * gain + bias
    return (jax.nn.silu(inner).astype(jnp.bfloat16), unit, inner, inv_std)


def norm_back(grad_act, unit, inner, inv_std, gain, groups):
    chans = grad_act.shape[3]
    members = clip_members(grad_act, groups)
    squash = jax.nn.sigmoid(inner)
    grad_inner = grad_act * squash * (1.0 + inner * (1.0 - squash))
    grad_gain, grad_bias = lax.psum(
        (jnp.sum(grad_inner * unit, axis=(0, 1, 2)), jnp.sum(grad_inner, axis=(0, 1, 2))),
        ("ta", "ha", "wa"),
    )
    first = jnp.repeat((gain * grad_bias).reshape(groups, -1).sum(1), chans // groups) / members
    second = jnp.repeat((gain * grad_gain).reshape(groups, -1).sum(1), chans // groups) / members
    grad_field = (grad_inner * gain - first - unit * second) * inv_std
    return (grad_field, grad_gain, grad_bias)


def pad_block(active, later):
    step_by = -1 if later else 1
    edge = active[:2] if later else active[-2:]
    moved = from_behind(edge, "ta", step_by)
    joined = jnp.concatenate([active, moved] if later else [moved, active], axis=0)
    return extended(joined, (("ha", 1), ("wa", 2)), 1)


def kernel_of(weights):
    chans = weights.shape[2]
    return weights.reshape(3, 3, 3, chans, chans)


def apply_kernel(padded, kernel):
    result = lax.conv_general_dilated(
        padded[None],
        kernel,
        (1, 1, 1),
        "VALID",
        dimension_numbers=("NDHWC", "DHWIO", "NDHWC"),
        preferred_element_type=jnp.float32,
    )
    return result[0]


def flipped_kernel(weights):
    return jnp.swapaxes(lax.rev(kernel_of(weights), (0, 1, 2)), 3, 4)


def shards(features, cotangent, conv_one, conv_two, gain_one, bias_one, gain_two, bias_two):
    groups = GROUPS
    act_one, unit_one, inner_one, inv_one = normalize(features, gain_one, bias_one, groups)
    whole_one, whole_two = (
        lax.all_gather(conv_one, ("ha", "wa"), axis=1, tiled=True),
        lax.all_gather(conv_two, ("ha", "wa"), axis=1, tiled=True),
    )
    hidden = apply_kernel(pad_block(act_one, False), kernel_of(whole_one))
    act_two, unit_two, inner_two, inv_two = normalize(hidden, gain_two, bias_two, groups)
    branch = apply_kernel(pad_block(act_two, False), kernel_of(whole_two))
    block_out = features + branch
    cotangent_low = cotangent.astype(jnp.bfloat16)
    grad_act_two = apply_kernel(pad_block(cotangent_low, True), flipped_kernel(whole_two))
    grad_hidden, gain_grad_two, bias_grad_two = norm_back(
        grad_act_two, unit_two, inner_two, inv_two, gain_two, groups
    )
    grad_act_one = apply_kernel(
        pad_block(grad_hidden.astype(jnp.bfloat16), True), flipped_kernel(whole_one)
    )
    grad_field, gain_grad_one, bias_grad_one = norm_back(
        grad_act_one, unit_one, inner_one, inv_one, gain_one, groups
    )
    grad_input = cotangent + grad_field
    norm_grads = jnp.stack([gain_grad_one, bias_grad_one, gain_grad_two, bias_grad_two])
    return (block_out, grad_input, norm_grads)


def solution(mesh):
    return jax.shard_map(
        shards,
        mesh=mesh,
        in_specs=(
            P("ta", "ha", "wa", None),
            P("ta", "ha", "wa", None),
            P(None, ("ha", "wa"), None),
            P(None, ("ha", "wa"), None),
            P(),
            P(),
            P(),
            P(),
        ),
        out_specs=(P("ta", "ha", "wa", None), P("ta", "ha", "wa", None), P()),
        check_vma=False,
    )
```

profile of v0, /device:TPU:1, one launch (start us, length us, event | category | flops | bytes accessed | tf_op | source)
XLA Modules:
  0.0 694.2 jit_solution(15843554134868363052)
XLA Ops:
  7.2 1.5 copy.36
  8.8 1.5 copy.42
  10.3 1.0 convert_element_type.14
  11.3 1.3 collective-permute-start.10
  12.6 1.0 reduce_sum.144
  13.7 108.5 %psum.56 = f32[32,8]{1,0:T(8,128)S(1)} all-reduce(f32[32,8]{1,0:T(8,128)S(1)} %reshape.96), channel_id=1, replica_groups=mesh['ta'=8,'ha'=8,'wa'=8] {'ta','ha','wa'}, use_global_device_ids=true, to_apply=%region_1.0 | all-reduce | flops 256 | bytes 2048 | tf_op jit(solution)/shard_map/psum | solution.py:39
  122.5 1.1 multiply_reduce_fusion.3
  123.7 94.3 %psum.57 = f32[32,8]{1,0:T(8,128)S(1)} all-reduce(f32[32,8]{1,0:T(8,128)S(1)} %reshape.97), channel_id=1, replica_groups=mesh['ta'=8,'ha'=8,'wa'=8] {'ta','ha','wa'}, use_global_device_ids=true, to_apply=%region_4.0 | all-reduce | flops 256 | bytes 2048 | tf_op jit(solution)/shard_map/psum | solution.py:42
  218.3 0.9 multiply_convert_fusion.2
  219.2 2.2 collective-permute-start
  221.4 1.4 collective-permute-start.11
  222.8 1.3 collective-permute-start.12
  224.2 4.5 collective-permute-start.1
  228.7 1.3 collective-permute-start.2
  230.1 5.4 collective-permute-start.13
  235.5 1.9 collective-permute-start.14
  237.5 3.6 collective-permute-start.3
  241.1 1.9 collective-permute-start.4
  243.1 0.3 maximum_bitcast_fusion.3
  243.4 0.2 copy.63
  243.6 0.2 pad.4.clone
  243.9 2.5 collective-permute-done.4
  246.4 0.3 maximum_bitcast_fusion
  246.8 0.2 copy.35
  247.2 2.8 copy.37
  250.0 1.6 select_reduce_fusion
  251.6 0.1 copy-done.2
  251.8 98.1 %psum.58 = f32[32,8]{1,0:T(8,128)S(1)} all-reduce(f32[32,8]{1,0:T(8,128)S(1)} %reshape.99), channel_id=1, replica_groups=mesh['ta'=8,'ha'=8,'wa'=8] {'ta','ha','wa'}, use_global_device_ids=true, to_apply=%region_7.8 | all-reduce | flops 256 | bytes 2048 | tf_op jit(solution)/shard_map/psum | solution.py:39
  350.2 2.8 copy.43
  353.1 1.7 convolution_select_fusion.1
  354.8 0.1 copy.49
  354.9 0.1 copy.38
  355.2 95.7 %psum.59 = f32[32,8]{1,0:T(8,128)S(1)} all-reduce(f32[32,8]{1,0:T(8,128)S(1)} %reshape.100), channel_id=1, replica_groups=mesh['ta'=8,'ha'=8,'wa'=8] {'ta','ha','wa'}, use_global_device_ids=true, to_apply=%region_10.11 | all-reduce | flops 256 | bytes 2048 | tf_op jit(solution)/shard_map/psum | solution.py:42
  451.2 0.2 fusion.53
  451.4 93.6 %all-reduce.1 = (f32[256]{0:T(256)S(1)}, f32[256]{0:T(256)S(1)}) all-reduce(f32[256]{0:T(256)S(1)} %get-tuple-element.12, f32[256]{0:T(256)S(1)} %get-tuple-element.11), channel_id=1, replica_groups=mesh['ta'=8,'ha'=8,'wa'=8] {'ta','ha','wa'}, use_global_device_ids=true, to_apply=%region_16.17 | all-reduce | flops 512 | bytes 4096 | tf_op jit(solution)/shard_map/psum | solution.py:55
  545.4 0.1 reduce_sum.155
  545.8 2.4 collective-permute-start.5
  548.3 1.3 collective-permute-start.15
  549.6 0.7 collective-permute-done.5
  550.4 2.4 collective-permute-start.6
  552.8 1.3 collective-permute-start.7
  554.2 4.2 collective-permute-start.16
  558.5 1.3 collective-permute-start.17
  559.8 5.9 collective-permute-start.8
  565.7 1.9 collective-permute-start.9
  567.7 3.6 collective-permute-start.18
  571.4 1.9 collective-permute-start.19
  573.3 0.3 maximum_bitcast_fusion.1
  573.8 0.2 copy.41
  573.9 2.7 collective-permute-done.19
  576.6 0.3 maximum_bitcast_fusion.2
  577.0 0.2 copy.52
  577.3 1.3 copy-done.3
  578.6 1.6 convolution_select_fusion
  580.2 0.1 copy.53
  580.4 0.2 fusion.52
  580.6 99.6 %all-reduce = (f32[256]{0:T(256)S(1)}, f32[256]{0:T(256)S(1)}) all-reduce(f32[256]{0:T(256)S(1)} %get-tuple-element.10, f32[256]{0:T(256)S(1)} %get-tuple-element.9), channel_id=1, replica_groups=mesh['ta'=8,'ha'=8,'wa'=8] {'ta','ha','wa'}, use_global_device_ids=true, to_apply=%region_22.23 | all-reduce | flops 512 | bytes 4096 | tf_op jit(solution)/shard_map/psum | solution.py:55
  680.7 0.1 reduce_sum.159
  681.1 3.6 convolution_select_fusion.2
  684.7 0.1 copy.44
  684.9 0.4 copy_add_fusion
  685.2 0.8 copy.56
  686.0 0.8 copy.55
  686.8 0.6 pad_maximum_fusion.24
  (99 shorter events, 4.2 us)
Async XLA Ops:
  7.2 211.1 %copy-start = (f32[2,8,16,256]{3,2,1,0:T(8,128)S(1)}, f32[2,8,16,256]{3,2,1,0:T(8,128)}, u32[]{:S(2)}) copy-start(f32[2,8,16,256]{3,2,1,0:T(8,128)} %param.8) | copy-start | bytes 786436
  7.2 240.0 %all-gather.3.cloned.1.call-start = ((), (), s32[]{:S(2)}) async-start(), calls=%async_computation | async-start | bytes 4792320 | tf_op jit(solution)/shard_map/all_gather | solution.py:98
  8.8 341.4 %all-gather.5.cloned.1.call-start = ((), (), s32[]{:S(2)}) async-start(), calls=%async_computation.1 | async-start | bytes 4792320 | tf_op jit(solution)/shard_map/all_gather | solution.py:99
  11.3 210.1 %collective-permute-start.10 = (bf16[2,8,16,256]{3,2,1,0:T(8,128)(2,1)S(1)}, bf16[2,8,16,256]{3,2,1,0:T(8,128)(2,1)S(1)}, u32[]{:S(2)}, u32[]{:S(2)}) collective-permute-start(bf16[2,8,16,256]{3,2,1,0:T(8,128)(2,1)S(1)} %convert_element_type.14), channel_id=1, source_target_pairs={{64,0},{128,64},{192,128},{256,192},{320,256},{384,320},{448,384},... | collective-permute-start | bytes 393224 | tf_op jit(solution)/shard_map/ppermute | solution.py:15
  219.2 4.9 collective-permute-start
  221.4 8.6 %collective-permute-start.11 = (bf16[4,1,16,256]{3,2,1,0:T(8,128)(2,1)S(1)}, bf16[4,1,16,256]{3,2,1,0:T(8,128)(2,1)S(1)}, u32[]{:S(2)}, u32[]{:S(2)}) collective-permute-start(bf16[4,1,16,256]{3,2,1,0:T(8,128)(2,1)S(1)} %get-tuple-element.32), channel_id=1, source_target_pairs={{0,8},{8,16},{16,24},{24,32},{32,40},{40,48},{48,56},{1,9},{9,17},... | collective-permute-start | bytes 98312 | tf_op jit(solution)/shard_map/ppermute | solution.py:23
  222.8 7.2 %collective-permute-start.12 = (bf16[4,1,16,256]{3,2,1,0:T(8,128)(2,1)S(1)}, bf16[4,1,16,256]{3,2,1,0:T(8,128)(2,1)S(1)}, u32[]{:S(2)}, u32[]{:S(2)}) collective-permute-start(bf16[4,1,16,256]{3,2,1,0:T(8,128)(2,1)S(1)} %get-tuple-element.33), channel_id=1, source_target_pairs={{8,0},{16,8},{24,16},{32,24},{40,32},{48,40},{56,48},{9,1},{17,9},... | collective-permute-start | bytes 98312 | tf_op jit(solution)/shard_map/ppermute | solution.py:26
  224.2 13.2 %collective-permute-start.1 = (bf16[4,1,16,256]{3,1,2,0:T(2,128)(2,1)S(1)}, bf16[4,1,16,256]{3,1,2,0:T(2,128)(2,1)S(1)}, u32[]{:S(2)}, u32[]{:S(2)}) collective-permute-start(bf16[4,1,16,256]{3,1,2,0:T(2,128)(2,1)S(1)} %get-tuple-element.36), channel_id=1, source_target_pairs={{0,8},{8,16},{16,24},{24,32},{32,40},{40,48},{48,56},{1,9},{9,17},... | collective-permute-start | bytes 98312 | tf_op jit(solution)/shard_map/ppermute | solution.py:23
  228.7 8.7 %collective-permute-start.2 = (bf16[4,1,16,256]{3,1,2,0:T(2,128)(2,1)S(1)}, bf16[4,1,16,256]{3,1,2,0:T(2,128)(2,1)S(1)}, u32[]{:S(2)}, u32[]{:S(2)}) collective-permute-start(bf16[4,1,16,256]{3,1,2,0:T(2,128)(2,1)S(1)} %get-tuple-element.37), channel_id=1, source_target_pairs={{8,0},{16,8},{24,16},{32,24},{40,32},{48,40},{56,48},{9,1},{17,9},... | collective-permute-start | bytes 98312 | tf_op jit(solution)/shard_map/ppermute | solution.py:26
  230.1 13.0 %collective-permute-start.13 = (bf16[4,10,1,256]{3,2,1,0:T(2,128)(2,1)S(1)}, bf16[4,10,1,256]{3,2,1,0:T(2,128)(2,1)S(1)}, u32[]{:S(2)}, u32[]{:S(2)}) collective-permute-start(bf16[4,10,1,256]{3,2,1,0:T(2,128)(2,1)S(1)} %get-tuple-element.26), channel_id=1, source_target_pairs={{0,1},{1,2},{2,3},{3,4},{4,5},{5,6},{6,7},{8,9},{9,10},{10,11},{11... | collective-permute-start | bytes 61448 | tf_op jit(solution)/shard_map/ppermute | solution.py:23
  235.5 7.6 %collective-permute-start.14 = (bf16[4,10,1,256]{3,2,1,0:T(2,128)(2,1)S(1)}, bf16[4,10,1,256]{3,2,1,0:T(2,128)(2,1)S(1)}, u32[]{:S(2)}, u32[]{:S(2)}) collective-permute-start(bf16[4,10,1,256]{3,2,1,0:T(2,128)(2,1)S(1)} %get-tuple-element.27), channel_id=1, source_target_pairs={{1,0},{2,1},{3,2},{4,3},{5,4},{6,5},{7,6},{9,8},{10,9},{11,10},{12... | collective-permute-start | bytes 61448 | tf_op jit(solution)/shard_map/ppermute | solution.py:26
  237.5 6.4 collective-permute-start.3
  241.1 5.2 collective-permute-start.4
  247.1 2.9 copy-start.9
  250.0 1.8 copy-start.2
  353.1 1.8 copy-start.1
  354.8 96.3 %copy-start.6 = (f32[256]{0:T(256)S(1)}, f32[256]{0:T(256)}, u32[]{:S(2)}) copy-start(f32[256]{0:T(256)} %param.14) | copy-start | bytes 3076
  354.8 96.4 %copy-start.8 = (f32[256]{0:T(256)S(1)}, f32[256]{0:T(256)}, u32[]{:S(2)}) copy-start(f32[256]{0:T(256)} %param.15) | copy-start | bytes 3076
  545.8 4.6 collective-permute-start.5
  548.3 5.9 collective-permute-start.15
  550.4 9.4 %collective-permute-start.6 = (bf16[4,1,16,256]{3,1,2,0:T(2,128)(2,1)S(1)}, bf16[4,1,16,256]{3,1,2,0:T(2,128)(2,1)S(1)}, u32[]{:S(2)}, u32[]{:S(2)}) collective-permute-start(bf16[4,1,16,256]{3,1,2,0:T(2,128)(2,1)S(1)} %get-tuple-element.34), channel_id=1, source_target_pairs={{0,8},{8,16},{16,24},{24,32},{32,40},{40,48},{48,56},{1,9},{9,17},... | collective-permute-start | bytes 98312 | tf_op jit(solution)/shard_map/ppermute | solution.py:23
  552.8 7.0 %collective-permute-start.7 = (bf16[4,1,16,256]{3,1,2,0:T(2,128)(2,1)S(1)}, bf16[4,1,16,256]{3,1,2,0:T(2,128)(2,1)S(1)}, u32[]{:S(2)}, u32[]{:S(2)}) collective-permute-start(bf16[4,1,16,256]{3,1,2,0:T(2,128)(2,1)S(1)} %get-tuple-element.35), channel_id=1, source_target_pairs={{8,0},{16,8},{24,16},{32,24},{40,32},{48,40},{56,48},{9,1},{17,9},... | collective-permute-start | bytes 98312 | tf_op jit(solution)/shard_map/ppermute | solution.py:26
  554.2 13.5 %collective-permute-start.16 = (bf16[4,1,16,256]{3,1,2,0:T(2,128)(2,1)S(1)}, bf16[4,1,16,256]{3,1,2,0:T(2,128)(2,1)S(1)}, u32[]{:S(2)}, u32[]{:S(2)}) collective-permute-start(bf16[4,1,16,256]{3,1,2,0:T(2,128)(2,1)S(1)} %get-tuple-element.30), channel_id=1, source_target_pairs={{0,8},{8,16},{16,24},{24,32},{32,40},{40,48},{48,56},{1,9},{9,17},... | collective-permute-start | bytes 98312 | tf_op jit(solution)/shard_map/ppermute | solution.py:23
  558.5 9.2 %collective-permute-start.17 = (bf16[4,1,16,256]{3,1,2,0:T(2,128)(2,1)S(1)}, bf16[4,1,16,256]{3,1,2,0:T(2,128)(2,1)S(1)}, u32[]{:S(2)}, u32[]{:S(2)}) collective-permute-start(bf16[4,1,16,256]{3,1,2,0:T(2,128)(2,1)S(1)} %get-tuple-element.31), channel_id=1, source_target_pairs={{8,0},{16,8},{24,16},{32,24},{40,32},{48,40},{56,48},{9,1},{17,9},... | collective-permute-start | bytes 98312 | tf_op jit(solution)/shard_map/ppermute | solution.py:26
  559.8 13.5 %collective-permute-start.8 = (bf16[4,10,1,256]{3,1,2,0:T(8,128)(2,1)S(1)}, bf16[4,10,1,256]{3,1,2,0:T(8,128)(2,1)S(1)}, u32[]{:S(2)}, u32[]{:S(2)}) collective-permute-start(bf16[4,10,1,256]{3,1,2,0:T(8,128)(2,1)S(1)} %get-tuple-element.22), channel_id=1, source_target_pairs={{0,1},{1,2},{2,3},{3,4},{4,5},{5,6},{6,7},{8,9},{9,10},{10,11},{11... | collective-permute-start | bytes 61448 | tf_op jit(solution)/shard_map/ppermute | solution.py:23
  565.7 7.6 %collective-permute-start.9 = (bf16[4,10,1,256]{3,1,2,0:T(8,128)(2,1)S(1)}, bf16[4,10,1,256]{3,1,2,0:T(8,128)(2,1)S(1)}, u32[]{:S(2)}, u32[]{:S(2)}) collective-permute-start(bf16[4,10,1,256]{3,1,2,0:T(8,128)(2,1)S(1)} %get-tuple-element.23), channel_id=1, source_target_pairs={{1,0},{2,1},{3,2},{4,3},{5,4},{6,5},{7,6},{9,8},{10,9},{11,10},{12... | collective-permute-start | bytes 61448 | tf_op jit(solution)/shard_map/ppermute | solution.py:26
  567.7 6.2 collective-permute-start.18
  571.4 5.2 collective-permute-start.19
  576.6 2.0 copy-start.3
  578.6 1.7 copy-start.5
  578.6 1.8 copy-start.7
  681.1 3.7 copy-start.4
Sparse Core Ops, SparseCore 0:
  11.9 90.8 all-gather.2
  106.7 82.2 all-gather.4
where the time goes:
time: 696 us; the launch traced here: 694 us
  blocking collectives  590 us (85%)
  starting transfers between devices  51.2 us (7%)
  local copies, waits for them, and re-layouts  15.7 us (2%)
  between operations  14.8 us (2%)
  matrix products  8.45 us (1%)
  other arithmetic  8.24 us (1%)
    psum x2, blocking collectives, normalize(): totals = lax.psum(jnp.sum(field, axis=(0, 1, 2)), ('ta', 'ha', 'wa'))  207 us
    psum x2, blocking collectives, norm_back(): lax.psum((jnp.sum(grad_inner * unit, axis=(0, 1, 2)), jnp.sum(grad_inner,...  193 us
    psum x2, blocking collectives, normalize(): lax.psum(jnp.sum(deviation * deviation, axis=(0, 1, 2)), ('ta', 'ha', 'wa'))  190 us
    ppermute x8, starting transfers between devices, extended(): lax.ppermute(lax.slice_in_dim(block, block.shape[dim] - width, None, axis...  31.1 us
  transfers between devices with their start and end apart: 22, of which 3 were waited for; matrix products, arithmetic and copies ran while one was open for 2% of the time, Pallas kernels for 0%

commit v1 on v0

v1 whole, which is shorter than its diff:
```python
import functools

import jax
import jax.numpy as jnp
from jax import lax
from jax.experimental import pallas as pl
from jax.experimental.pallas import tpu as pltpu
from jax.sharding import PartitionSpec as P

AXES = ("ta", "ha", "wa")
N = 8
C = 256
GROUP = 8
EPS = 1e-06
CELLS = 256
MESH = pl.DeviceIdType.MESH
F32 = jnp.float32
BF16 = jnp.bfloat16

FEAT, COT, HID, GRAD = range(4)
OWN = {FEAT: 2, COT: 0, HID: 2, GRAD: 0}
STEPS = {FEAT: (0, 1), COT: (0, -1), HID: (0, -1, 1), GRAD: (0, -1)}


def sigmoid(v):
    return 1.0 / (1.0 + jnp.exp(-v))


def group_sum(v):
    lane = lax.broadcasted_iota(jnp.int32, v.shape, 1)
    for s in (1, 2, 4):
        up = pltpu.roll(v, s, 1)
        down = pltpu.roll(v, C - s, 1)
        v = v + jnp.where((lane & s) != 0, up, down)
    return v


def kernel(
    feat, cot, w_one, w_two, gain_one, bias_one, gain_two, bias_two,
    block_out, grad_input, norm_grads,
    fx, cx, hx, gx, fk, ck, hk, gk, fq, cq, hq, gq, ks, qs,
    lhs_a, lhs_b, xs, xb, wb, stage, board, inner_grad, unit_buf, ga,
    local_sem, ar_s, ar_r, halo_s, halo_r, x_s, x_r, ring_s, ring_r, sib_s, sib_r,
):
    ta, ha, wa = (lax.axis_index(a) for a in AXES)
    me = (ta, ha, wa)
    core = lax.rem(wa, 2)
    sibling = (ta, ha, wa + 1 - 2 * core)
    fields = {FEAT: fx, COT: cx, HID: hx, GRAD: gx}
    cols = {FEAT: fk, COT: ck, HID: hk, GRAD: gk}
    corners = {FEAT: fq, COT: cq, HID: hq, GRAD: gq}

    def along(axis, k):
        spot = list(me)
        spot[axis] = lax.rem(me[axis] + k, N)
        return tuple(spot)

    barrier = pltpu.get_barrier_semaphore()
    count = 0
    for axis in range(3):
        for k in range(1, N):
            pl.semaphore_signal(barrier, inc=1, device_id=along(axis, k), device_id_type=MESH)
            count += 1
    for dt in (-1, 0, 1):
        for dh in (-1, 0, 1):
            for dw in (-1, 0, 1):
                if abs(dt) + abs(dh) + abs(dw) >= 2:
                    spot = tuple(lax.rem(m + d + N, N) for m, d in zip(me, (dt, dh, dw)))
                    pl.semaphore_signal(barrier, inc=1, device_id=spot, device_id_type=MESH)
                    count += 1

    load_f = pltpu.make_async_copy(feat, fx.at[pl.ds(2, 2), pl.ds(1, 8)], local_sem.at[0])
    load_c = pltpu.make_async_copy(cot, cx.at[pl.ds(0, 2), pl.ds(1, 8)], local_sem.at[1])
    load_f.start()
    load_c.start()

    def reduce_copies(k, s):
        axis = 2 - s
        return [
            pltpu.make_async_remote_copy(
                src_ref=stage.at[k, s],
                dst_ref=board.at[k, s, me[axis]],
                send_sem=ar_s.at[k, s],
                recv_sem=ar_r.at[k, s],
                device_id=along(axis, j),
                device_id_type=MESH,
            )
            for j in (4, 3, 5, 2, 6, 1, 7)
        ]

    def reduce_send(k, s, value):
        stage[k, s] = value
        board[k, s, me[2 - s]] = value
        for copy in reduce_copies(k, s):
            copy.start()

    def reduce_get(k, s):
        seven = board.at[k, s, pl.ds(0, N - 1)]
        pltpu.make_async_copy(seven, seven, ar_r.at[k, s]).wait()
        return board[k, s]

    def merge_moments(k, s):
        got = reduce_get(k, s)
        cells = float(CELLS * N**s)
        means, squares = got[:, 0:1, :], got[:, 1:2, :]
        mean = jnp.sum(means, axis=0) * (1.0 / N)
        off = means - mean[None]
        square = jnp.sum(squares, axis=0) + cells * jnp.sum(off * off, axis=0)
        return jnp.concatenate([mean, square], axis=0)

    def merge_sums(k, s):
        return jnp.sum(reduce_get(k, s), axis=0)

    def local_moments(ref, own):
        v = ref[pl.ds(own, 2), pl.ds(1, 8)].reshape(CELLS, C)
        mean = jnp.sum(v, axis=0, keepdims=True) * (1.0 / CELLS)
        d = v - mean
        return jnp.concatenate([mean, jnp.sum(d * d, axis=0, keepdims=True)], axis=0)

    def finish_moments(pair):
        cells = float(CELLS * N**3)
        mean, square = pair[0:1], pair[1:2]
        centre = group_sum(mean) * (1.0 / GROUP)
        off = mean - centre
        spread = group_sum(square + cells * off * off) * (1.0 / (cells * GROUP))
        return centre, 1.0 / jnp.sqrt(spread + EPS)

    def halo_messages(field):
        own, x, k, q = OWN[field], fields[field], cols[field], corners[field]
        src_t = pl.ds(own, 2)
        for dt in STEPS[field]:
            dst_t = pl.ds(own - 2 * dt, 2)
            for dh in (0, -1, 1):
                for dw in (0, -1, 1):
                    if (dt, dh, dw) == (0, 0, 0):
                        continue
                    r, b = int(dw > 0), int(dh > 0)
                    if dh == 0 and dw == 0:
                        src, dst = x.at[src_t, pl.ds(1, 8)], x.at[dst_t, pl.ds(1, 8)]
                    elif dw == 0:
                        src, dst = x.at[src_t, 8 if b else 1], x.at[dst_t, 0 if b else 9]
                    elif dh == 0:
                        src, dst = ks.at[field, r], k.at[1 - r, dst_t]
                    else:
                        src, dst = qs.at[field, r, b], q.at[1 - r, 1 - b, dst_t]
                    spot = (ta + dt, ha + dh, wa + dw)
                    back = (ta - dt, ha - dh, wa - dw)
                    number = (dt + 1) * 9 + (dh + 1) * 3 + dw + 1
                    copy = pltpu.make_async_remote_copy(
                        src_ref=src, dst_ref=dst,
                        send_sem=halo_s.at[field, number], recv_sem=halo_r.at[field, number],
                        device_id=spot, device_id_type=MESH,
                    )
                    yield copy, inside(spot, (dt, dh, dw)), inside(back, (-dt, -dh, -dw))

    def inside(spot, delta):
        ok = None
        for v, d in zip(spot, delta):
            if d:
                one = v < N if d > 0 else v >= 0
                ok = one if ok is None else jnp.logical_and(ok, one)
        return ok

    def halo_send(field):
        own, x = OWN[field], fields[field]
        for r, w in ((0, 0), (1, 15)):
            for t in range(2):
                for h in range(8):
                    row = x[own + t, 1 + h, w : w + 1, :]
                    ks[field, r, t, h : h + 1, :] = row
                    if h in (0, 7):
                        qs[field, r, h // 7, t] = row
        for copy, goes, _ in halo_messages(field):
            pl.when(goes)(copy.start)

    def halo_wait(field):
        for copy, _, comes in halo_messages(field):
            pl.when(comes)(copy.wait_recv)

    def halo_done(field):
        for copy, goes, _ in halo_messages(field):
            pl.when(goes)(copy.wait_send)

    shift = 4 * lax.rem(wa, 4)

    def shard_stage(conv, ref):
        for a in range(3):
            rows = jnp.concatenate([ref[a].astype(F32), jnp.zeros((12, C), F32)], axis=0)
            rows = pltpu.roll(rows, shift, 0).astype(BF16)
            xs[conv, a] = rows
            xb[conv, wa, a] = rows

    def shard_copies(conv):
        return [
            pltpu.make_async_remote_copy(
                src_ref=xs.at[conv], dst_ref=xb.at[conv, wa],
                send_sem=x_s.at[conv], recv_sem=x_r.at[conv],
                device_id=along(2, j), device_id_type=MESH,
            )
            for j in range(1, N)
        ]

    def shard_send(conv):
        for copy in shard_copies(conv):
            copy.start()

    def shard_merge(conv):
        seven = xb.at[conv, pl.ds(0, N - 1)]
        pltpu.make_async_copy(seven, seven, x_r.at[conv]).wait()
        for a in range(3):
            for g in range(2):
                parts = [[xb[conv, 4 * g + p, a, 16 * i : 16 * i + 16, :] for i in range(3)] for p in range(4)]
                tiles = [parts[0][0], parts[0][1]]
                for p in range(1, 4):
                    tiles.append(parts[p - 1][2] + parts[p][0])
                    tiles.append(parts[p][1])
                tiles.append(parts[3][2])
                for i, tile in enumerate(tiles):
                    wb[conv, a, 18 * ha + 9 * g + i] = tile

    def piece(conv, way, step, half):
        block = lax.rem(ha - step + N, N) if way == 0 else lax.rem(ha + step, N)
        taps = pl.ds(0, 3) if step < 4 else (pl.ds(0, 2) if way == 0 else pl.ds(2, 1))
        return wb.at[conv, taps, pl.ds(18 * block + 9 * half, 9)]

    def ring_copy(conv, way, step):
        block = lax.rem(ha - (step - 1) + N, N) if way == 0 else lax.rem(ha + step - 1, N)
        taps = pl.ds(0, 3) if step < 4 else (pl.ds(0, 2) if way == 0 else pl.ds(2, 1))
        ref = wb.at[conv, taps, pl.ds(18 * block + 9 * core, 9)]
        return pltpu.make_async_remote_copy(
            src_ref=ref, dst_ref=ref,
            send_sem=ring_s.at[conv, way, step - 1], recv_sem=ring_r.at[conv, way, step - 1],
            device_id=along(1, 1 if way == 0 else N - 1), device_id_type=MESH,
        )

    def sibling_copy(conv, way, step):
        ref = piece(conv, way, step, core)
        return pltpu.make_async_remote_copy(
            src_ref=ref, dst_ref=ref,
            send_sem=sib_s.at[conv, way, step - 1], recv_sem=sib_r.at[conv, way, step - 1],
            device_id=sibling, device_id_type=MESH,
        )

    def ring_start(conv):
        for way in (0, 1):
            ring_copy(conv, way, 1).start()

    def ring_step(conv, step):
        for way in (0, 1):
            got = piece(conv, way, step, core)
            pltpu.make_async_copy(got, got, ring_r.at[conv, way, step - 1]).wait()
            if step < 4:
                ring_copy(conv, way, step + 1).start()
            sibling_copy(conv, way, step).start()

    def sibling_wait(conv):
        for step in range(1, 5):
            for way in (0, 1):
                got = piece(conv, way, step, 1 - core)
                pltpu.make_async_copy(got, got, sib_r.at[conv, way, step - 1]).wait()

    def weights_done(conv):
        for copy in shard_copies(conv):
            copy.wait_send()
        for step in range(1, 5):
            for way in (0, 1):
                ring_copy(conv, way, step).wait_send()
                sibling_copy(conv, way, step).wait_send()

    row_of = lax.broadcasted_iota(jnp.int32, (16, C), 0)

    def fill(lhs, refs, first, early, late, fn, flip):
        groups = [tuple(r[0] for r in refs), tuple(r[1] for r in refs), tuple(r[2] for r in refs)]
        xs_, ks_, qs_ = groups
        top, bottom, left, right = ha > 0, ha < N - 1, wa > 0, wa < N - 1

        def body(t, carry):
            src = t + first
            frame = jnp.logical_and(jnp.logical_or(t >= 2, early), jnp.logical_or(t < 2, late))
            sides = []
            for r, ok in ((0, left), (1, right)):
                ok = jnp.logical_and(ok, frame)
                mid = jnp.where(ok, fn(*[k[r, src] for k in ks_]), 0.0)
                hi = jnp.where(jnp.logical_and(ok, top), fn(*[q[r, 0, src] for q in qs_]), 0.0)
                lo = jnp.where(jnp.logical_and(ok, bottom), fn(*[q[r, 1, src] for q in qs_]), 0.0)
                sides.append([hi] + [mid[h : h + 1] for h in range(8)] + [lo])
            for h in range(10):
                ok = frame
                if h == 0:
                    ok = jnp.logical_and(ok, top)
                if h == 9:
                    ok = jnp.logical_and(ok, bottom)
                v = jnp.where(ok, fn(*[x[src, h] for x in xs_]), 0.0)
                before = jnp.where(row_of == 0, sides[0][h], pltpu.roll(v, 1, 0))
                after = jnp.where(row_of == 15, sides[1][h], pltpu.roll(v, 15, 0))
                if flip:
                    before, after = after, before
                lhs[t, h, :, 0:C] = before.astype(BF16)
                lhs[t, h, :, C : 2 * C] = v.astype(BF16)
                lhs[t, h, :, 2 * C : 3 * C] = after.astype(BF16)
            return carry

        lax.fori_loop(0, 4, body, 0)

    def convolve(lhs, conv, flip):
        total = None
        for a in range(3):
            for b in range(3):
                part = lhs[a : a + 2, b : b + 8].reshape(CELLS, 3 * C)
                if flip:
                    w = wb[conv, 2 - a, pl.ds(48 * (2 - b), 48)].reshape(3 * C, C)
                    out = None
                    for c in range(3):
                        one = lax.dot_general(
                            part[:, c * C : c * C + C], w[c * C : c * C + C, :],
                            (((1,), (1,)), ((), ())), preferred_element_type=F32,
                        )
                        out = one if out is None else out + one
                else:
                    w = wb[conv, a, pl.ds(48 * b, 48)].reshape(3 * C, C)
                    out = jnp.dot(part, w, preferred_element_type=F32)
                total = out if total is None else total + out
        return total.reshape(2, 8, 16, C)

    shard_stage(0, w_one)
    shard_stage(1, w_two)
    load_f.wait()
    moments = local_moments(fx, 2)
    pl.semaphore_wait(barrier, count)
    reduce_send(0, 0, moments)
    shard_send(0)
    halo_send(FEAT)
    shard_send(1)
    load_c.wait()
    halo_send(COT)
    reduce_send(0, 1, merge_moments(0, 0))
    shard_merge(0)
    ring_start(0)
    reduce_send(0, 2, merge_moments(0, 1))
    shard_merge(1)
    ring_step(0, 1)
    ring_start(1)
    centre_1, inv_1 = finish_moments(merge_moments(0, 2))
    g1, b1, g2, b2 = gain_one[...], bias_one[...], gain_two[...], bias_two[...]
    halo_wait(FEAT)

    def act_one(v):
        inner = (v - centre_1) * inv_1 * g1 + b1
        return inner * sigmoid(inner)

    fill(lhs_a, [(fx, fk, fq)], 0, ta > 0, True, act_one, False)
    ring_step(0, 2)
    halo_wait(COT)
    fill(lhs_b, [(cx, ck, cq)], 0, True, ta < N - 1, lambda v: v, True)
    ring_step(0, 3)
    ring_step(0, 4)
    sibling_wait(0)

    hx[pl.ds(2, 2), pl.ds(1, 8)] = convolve(lhs_a, 0, False)
    reduce_send(1, 0, local_moments(hx, 2))
    halo_send(HID)
    ring_step(1, 1)
    reduce_send(1, 1, merge_moments(1, 0))
    ring_step(1, 2)
    reduce_send(1, 2, merge_moments(1, 1))
    ring_step(1, 3)
    ring_step(1, 4)
    sibling_wait(1)
    gx[pl.ds(0, 2), pl.ds(1, 8)] = convolve(lhs_b, 1, True)
    halo_send(GRAD)
    centre_2, inv_2 = finish_moments(merge_moments(1, 2))

    def back_sums(field, own, grad, centre, inv, gain, bias):
        def body(i, carry):
            gain_sum, bias_sum = carry
            t, h = i // 8, i % 8
            unit = (field[own + t, 1 + h] - centre) * inv
            inner = unit * gain + bias
            s = sigmoid(inner)
            gi = grad(t, h) * s * (1.0 + inner * (1.0 - s))
            inner_grad[i] = gi
            unit_buf[i] = unit
            return gain_sum + gi * unit, bias_sum + gi

        zero = jnp.zeros((16, C), F32)
        sums = lax.fori_loop(0, 16, body, (zero, zero))
        return jnp.concatenate([jnp.sum(s, axis=0, keepdims=True) for s in sums], axis=0)

    reduce_send(2, 0, back_sums(hx, 2, lambda t, h: gx[t, 1 + h], centre_2, inv_2, g2, b2))
    halo_wait(HID)

    def act_two(v):
        inner = (v - centre_2) * inv_2 * g2 + b2
        return inner * sigmoid(inner)

    fill(lhs_a, [(hx, hk, hq)], 0, ta > 0, True, act_two, False)
    reduce_send(2, 1, merge_sums(2, 0))
    block_out[...] = fx[pl.ds(2, 2), pl.ds(1, 8)] + convolve(lhs_a, 1, False)
    reduce_send(2, 2, merge_sums(2, 1))
    halo_wait(GRAD)
    sums_2 = merge_sums(2, 2)
    norm_grads[2:4, :] = sums_2
    members = float(CELLS * N**3 * GROUP)
    both = group_sum(sums_2 * g2) * (1.0 / members)
    first_2, second_2 = both[1:2], both[0:1]

    def grad_hidden(v, g):
        unit = (v - centre_2) * inv_2
        inner = unit * g2 + b2
        s = sigmoid(inner)
        gi = g * s * (1.0 + inner * (1.0 - s))
        return (gi * g2 - first_2 - unit * second_2) * inv_2

    class Shifted:
        def __init__(self, ref, lead):
            self.ref, self.lead = ref, lead

        def __getitem__(self, idx):
            idx = idx if isinstance(idx, tuple) else (idx,)
            n = self.lead
            return self.ref[idx[:n] + (idx[n] + 2,) + idx[n + 1 :]]

    fill(
        lhs_b,
        [(Shifted(hx, 0), Shifted(hk, 1), Shifted(hq, 2)), (gx, gk, gq)],
        0, True, ta < N - 1, grad_hidden, True,
    )
    grad_act = convolve(lhs_b, 0, True)
    ga[...] = grad_act

    reduce_send(3, 0, back_sums(fx, 2, lambda t, h: ga[t, h], centre_1, inv_1, g1, b1))
    for field in (FEAT, COT, HID):
        halo_done(field)
    reduce_send(3, 1, merge_sums(3, 0))
    for conv in (0, 1):
        weights_done(conv)
    reduce_send(3, 2, merge_sums(3, 1))
    halo_done(GRAD)
    sums_1 = merge_sums(3, 2)
    norm_grads[0:2, :] = sums_1
    both = group_sum(sums_1 * g1) * (1.0 / members)
    first_1, second_1 = both[1:2], both[0:1]

    def last(i, carry):
        t, h = i // 8, i % 8
        field = (inner_grad[i] * g1 - first_1 - unit_buf[i] * second_1) * inv_1
        grad_input[t, h] = cx[t, 1 + h] + field
        return carry

    lax.fori_loop(0, 16, last, 0)
    for k in range(4):
        for s in range(3):
            for copy in reduce_copies(k, s):
                copy.wait_send()


def shards(features, cotangent, conv_one, conv_two, gain_one, bias_one, gain_two, bias_two):
    vmem = pl.BlockSpec(memory_space=pltpu.VMEM)
    anywhere = pl.BlockSpec(memory_space=pl.ANY)

    def buf(*shape, dtype=F32):
        return pltpu.VMEM(shape, dtype)

    scratch = (
        [buf(t, 10, 16, C) for t in (4, 4, 6, 4)]
        + [buf(2, t, 8, C) for t in (4, 4, 6, 4)]
        + [buf(2, 2, t, 1, C) for t in (4, 4, 6, 4)]
        + [buf(4, 2, 2, 8, C), buf(4, 2, 2, 2, 1, C)]
        + [buf(4, 10, 16, 3 * C, dtype=BF16)] * 2
        + [buf(2, 3, 48, C, dtype=BF16), buf(2, N, 3, 48, C, dtype=BF16)]
        + [buf(2, 3, 144, 16, C, dtype=BF16)]
        + [buf(4, 3, 2, C), buf(4, 3, N, 2, C)]
        + [buf(16, 16, C)] * 2
        + [buf(2, 8, 16, C)]
        + [pltpu.SemaphoreType.DMA((2,))]
        + [pltpu.SemaphoreType.DMA((4, 3))] * 2
        + [pltpu.SemaphoreType.DMA((4, 27))] * 2
        + [pltpu.SemaphoreType.DMA((2,))] * 2
        + [pltpu.SemaphoreType.DMA((2, 2, 4))] * 4
    )
    block = jax.ShapeDtypeStruct((2, 8, 16, C), F32)
    return pl.pallas_call(
        kernel,
        out_shape=(block, block, jax.ShapeDtypeStruct((4, C), F32)),
        in_specs=[anywhere] * 2 + [vmem] * 6,
        out_specs=(vmem, vmem, vmem),
        scratch_shapes=scratch,
        compiler_params=pltpu.CompilerParams(
            collective_id=0, has_side_effects=True, vmem_limit_bytes=56 * 2**20
        ),
    )(
        features, cotangent, conv_one, conv_two,
        gain_one[None], bias_one[None], gain_two[None], bias_two[None],
    )


def solution(mesh):
    return jax.shard_map(
        shards,
        mesh=mesh,
        in_specs=(
            P("ta", "ha", "wa", None),
            P("ta", "ha", "wa", None),
            P(None, ("ha", "wa"), None),
            P(None, ("ha", "wa"), None),
            P(),
            P(),
            P(),
            P(),
        ),
        out_specs=(P("ta", "ha", "wa", None), P("ta", "ha", "wa", None), P()),
        check_vma=False,
    )
```

time: 696 us -> 117 us (0.17)
  blocking collectives: 590 us -> 0 us
  Pallas kernels: 0 us -> 113 us
  starting transfers between devices: 51.2 us -> 0 us
  between operations: 14.8 us -> 0.65 us
  local copies, waits for them, and re-layouts: 15.7 us -> 3.02 us
  matrix products: 8.45 us -> 0 us
  other arithmetic: 8.24 us -> 0 us
    psum x6 -> x0, blocking collectives: 590 us -> none  [the longest x2 207 us: normalize(): totals = lax.psum(jnp.sum(field, axis=(0, 1, 2)), ('ta', 'ha', 'wa'))]
    pallas_call x0 -> x1, Pallas kernels: none -> 113 us  [shards(): pl.pallas_call(kernel, out_shape=(block, block, jax.ShapeDtypeStruct((4,...]
    ppermute x20 -> x0, starting transfers between devices: 51.1 us -> none  [the longest x8 31.1 us: extended(): lax.ppermute(lax.slice_in_dim(block, block.shape[dim] - width, None, axis...]
    conv_general_dilated x4 -> x0, matrix products: 8.45 us -> none  [apply_kernel(): lax.conv_general_dilated(padded[None], kernel, (1, 1, 1), 'VALID', dimens...]
  transfers between devices with their start and end apart: 22 -> 0, of which waited for: 3 -> 0; matrix products, arithmetic and copies ran while one was open for 2% -> 0% of each run, Pallas kernels for 0% -> 0%
where the time goes in v1:
time: 117 us
  Pallas kernels  113 us (97%)
  local copies, waits for them, and re-layouts  3.02 us (3%)
    pallas_call x1, Pallas kernels, shards(): pl.pallas_call(kernel, out_shape=(block, block, jax.ShapeDtypeStruct((4,...  113 us
    unnamed x7, local copies, waits for them, and re-layouts  3.02 us

profile of v1, /device:TPU:1, one launch (start us, length us, event | category | flops | bytes accessed | tf_op | source)
XLA Modules:
  0.0 116.6 jit_solution(14731291380103228442)
XLA Ops:
  0.6 112.9 %shard_map.103 = (f32[2,8,16,256]{3,2,1,0:T(8,128)}, f32[2,8,16,256]{3,2,1,0:T(8,128)}, f32[4,256]{1,0:T(4,128)}) custom-call(f32[2,8,16,256]{3,2,1,0:T(8,128)} %feat.1, f32[2,8,16,256]{3,2,1,0:T(8,128)} %cot.1, bf16[3,36,256]{2,1,0:T(8,128)(2,1)} %w_one.1, bf16[3,36,256]{2,1,0:T(8,128)(2,1)} %w_two.1, f32[1,256]{1,0:T(1,128)} %bitcast.4, f32[1,256]{1,0:T(1,128)} %bitcast.5, ...), custom_call_target="tpu_custom_call" | custom-call | tf_op jit(solution)/shard_map/pallas_call | solution.py:482
  113.6 0.0 copy-start
  113.6 1.7 %copy.14 = f32[2,8,16,256]{3,2,1,0:T(8,128)} copy(f32[2,8,16,256]{3,2,1,0:T(8,128)} %get-tuple-element.6) | data formatting | bytes 524288
  115.3 0.0 copy-done
  115.3 0.0 copy-start.1
  115.3 0.7 copy.15
  116.0 0.0 copy-done.1
  116.0 0.6 copy.16
Async XLA Ops:
  113.6 1.7 %copy-start = (f32[2,8,16,256]{3,2,1,0:T(8,128)S(1)}, f32[2,8,16,256]{3,2,1,0:T(8,128)}, u32[]{:S(2)}) copy-start(f32[2,8,16,256]{3,2,1,0:T(8,128)} %get-tuple-element.7) | copy-start | bytes 786436
  115.3 0.7 copy-start.1

commit v2 on v1

v2 whole, which is shorter than its diff:
```python
import functools

import jax
import jax.numpy as jnp
from jax import lax
from jax.experimental import pallas as pl
from jax.experimental.pallas import tpu as pltpu
from jax.sharding import PartitionSpec as P

AXES = ("ta", "ha", "wa")
N = 8
C = 256
GROUP = 8
NEAR = (1, 7, 2, 6, 3, 5, 4)
EPS = 1e-06
CELLS = 256
MESH = pl.DeviceIdType.MESH
F32 = jnp.float32
BF16 = jnp.bfloat16

FEAT, HID, GRAD, COT, ACT = range(5)
NARROW = (COT, ACT)
OWN = {FEAT: 2, HID: 0, GRAD: 0, COT: 0, ACT: 2}


def sigmoid(v):
    return 1.0 / (1.0 + jnp.exp(-v))


def group_sum(v):
    lane = lax.broadcasted_iota(jnp.int32, v.shape, 1)
    for s in (1, 2, 4):
        up = pltpu.roll(v, s, 1)
        down = pltpu.roll(v, C - s, 1)
        v = v + jnp.where((lane & s) != 0, up, down)
    return v


def kernel(
    feat, cot, w_one, w_two, gain_one, bias_one, gain_two, bias_two,
    block_out, grad_input, norm_grads,
    cx, fx, hx, gx, nx, mx, fk, hk, gk, nk, mk, fq, hq, gq, nq, mq, ks, qs, ns, ms,
    lhs_a, lhs_b, shards_in, wb, stage, board, inner_grad, unit_buf, ga,
    local_sem, ar_s, ar_r, halo_s, halo_r, y_s, y_r, x_s, x_r, z_s, z_r, c_s, c_r,
):
    ta, ha, wa = (lax.axis_index(a) for a in AXES)
    me = (ta, ha, wa)
    core = lax.rem(wa, 2)
    sibling = (ta, ha, wa + 1 - 2 * core)
    fields = {FEAT: fx, HID: hx, GRAD: gx, COT: nx, ACT: mx}
    cols = {FEAT: fk, HID: hk, GRAD: gk, COT: nk, ACT: mk}
    corners = {FEAT: fq, HID: hq, GRAD: gq, COT: nq, ACT: mq}

    def along(axis, k):
        spot = list(me)
        spot[axis] = lax.rem(me[axis] + k, N)
        return tuple(spot)

    barrier = pltpu.get_barrier_semaphore()
    count = 0
    for axis in range(3):
        for k in range(1, N):
            pl.semaphore_signal(barrier, inc=1, device_id=along(axis, k), device_id_type=MESH)
            count += 1
    for dt in (-1, 0, 1):
        for dh in (-1, 0, 1):
            for dw in (-1, 0, 1):
                if abs(dt) + abs(dh) + abs(dw) >= 2:
                    spot = tuple(lax.rem(m + d + N, N) for m, d in zip(me, (dt, dh, dw)))
                    pl.semaphore_signal(barrier, inc=1, device_id=spot, device_id_type=MESH)
                    count += 1

    load_f = pltpu.make_async_copy(feat, fx.at[pl.ds(2, 2), pl.ds(1, 8)], local_sem.at[0])
    load_c = pltpu.make_async_copy(cot, cx, local_sem.at[1])
    load_f.start()
    load_c.start()

    def reduce_copies(k, s):
        axis = 2 - s
        return [
            pltpu.make_async_remote_copy(
                src_ref=stage.at[k, s],
                dst_ref=board.at[k, s, me[axis]],
                send_sem=ar_s.at[k, s],
                recv_sem=ar_r.at[k, s],
                device_id=along(axis, j),
                device_id_type=MESH,
            )
            for j in (4, 3, 5, 2, 6, 1, 7)
        ]

    def reduce_send(k, s, value):
        stage[k, s] = value
        board[k, s, me[2 - s]] = value
        for copy in reduce_copies(k, s):
            copy.start()

    def reduce_get(k, s):
        seven = board.at[k, s, pl.ds(0, N - 1)]
        pltpu.make_async_copy(seven, seven, ar_r.at[k, s]).wait()
        return board[k, s]

    def merge_moments(k, s):
        got = reduce_get(k, s)
        cells = float(CELLS * N**s)
        means, squares = got[:, 0:1, :], got[:, 1:2, :]
        mean = jnp.sum(means, axis=0) * (1.0 / N)
        off = means - mean[None]
        square = jnp.sum(squares, axis=0) + cells * jnp.sum(off * off, axis=0)
        return jnp.concatenate([mean, square], axis=0)

    def merge_sums(k, s):
        return jnp.sum(reduce_get(k, s), axis=0)

    def local_moments(ref, own):
        v = ref[pl.ds(own, 2), pl.ds(1, 8)].reshape(CELLS, C)
        mean = jnp.sum(v, axis=0, keepdims=True) * (1.0 / CELLS)
        d = v - mean
        return jnp.concatenate([mean, jnp.sum(d * d, axis=0, keepdims=True)], axis=0)

    def finish_moments(pair):
        cells = float(CELLS * N**3)
        mean, square = pair[0:1], pair[1:2]
        centre = group_sum(mean) * (1.0 / GROUP)
        off = mean - centre
        spread = group_sum(square + cells * off * off) * (1.0 / (cells * GROUP))
        return centre, 1.0 / jnp.sqrt(spread + EPS)

    def halo_messages(field):
        own, x, k, q = OWN[field], fields[field], cols[field], corners[field]
        src_t = pl.ds(own, 2)
        narrow = field in NARROW
        for dt in (0, 1 if own else -1):
            dst_t = pl.ds(own - 2 * dt, 2)
            dst_k = (own - 2 * dt) // 2 if narrow else dst_t
            for dh in (0, -1, 1):
                for dw in (0, -1, 1):
                    if (dt, dh, dw) == (0, 0, 0):
                        continue
                    r, b = int(dw > 0), int(dh > 0)
                    if dh == 0 and dw == 0:
                        src, dst = x.at[src_t, pl.ds(1, 8)], x.at[dst_t, pl.ds(1, 8)]
                    elif dw == 0:
                        src, dst = x.at[src_t, 8 if b else 1], x.at[dst_t, 0 if b else 9]
                    elif dh == 0:
                        src = ns.at[field - COT, r] if narrow else ks.at[field, r]
                        dst = k.at[1 - r, dst_k]
                    else:
                        src = ms.at[field - COT, r, b] if narrow else qs.at[field, r, b]
                        dst = q.at[1 - r, 1 - b, dst_k]
                    spot = (ta + dt, ha + dh, wa + dw)
                    back = (ta - dt, ha - dh, wa - dw)
                    number = (dt + 1) * 9 + (dh + 1) * 3 + dw + 1
                    copy = pltpu.make_async_remote_copy(
                        src_ref=src, dst_ref=dst,
                        send_sem=halo_s.at[field, number], recv_sem=halo_r.at[field, number],
                        device_id=spot, device_id_type=MESH,
                    )
                    yield copy, inside(spot, (dt, dh, dw)), inside(back, (-dt, -dh, -dw))

    def inside(spot, delta):
        ok = None
        for v, d in zip(spot, delta):
            if d:
                one = v < N if d > 0 else v >= 0
                ok = one if ok is None else jnp.logical_and(ok, one)
        return ok

    def halo_send(field):
        own, x = OWN[field], fields[field]
        for r, w in ((0, 0), (1, 15)):
            if field in NARROW:
                ns[field - COT, r] = x[own : own + 2, 1:9, w, :].astype(F32).reshape(16, C).astype(BF16)
                for b, h in ((0, 1), (1, 8)):
                    pair = [x[own + t, h, w : w + 1, :].astype(F32) for t in range(2)]
                    ms[field - COT, r, b] = jnp.concatenate(pair + [jnp.zeros((14, C), F32)], axis=0).astype(BF16)
                continue
            for t in range(2):
                for h in range(8):
                    row = x[own + t, 1 + h, w : w + 1, :]
                    ks[field, r, t, h : h + 1, :] = row
                    if h in (0, 7):
                        qs[field, r, h // 7, t] = row
        for copy, goes, _ in halo_messages(field):
            pl.when(goes)(copy.start)

    def halo_wait(field):
        for copy, _, comes in halo_messages(field):
            pl.when(comes)(copy.wait_recv)

    def halo_done(field):
        for copy, goes, _ in halo_messages(field):
            pl.when(goes)(copy.wait_send)

    shift = 4 * lax.rem(wa, 4)
    half = lax.rem(ta, 2)
    column = lax.div(wa, 2)

    def block(j):
        return lax.rem(ha - j + N, N)

    row_half = lax.broadcasted_iota(jnp.int32, (16, C // 2), 0)

    def shard_stage(conv, ref):
        spare = None
        for a in range(3):
            rows = jnp.concatenate([ref[a].astype(F32), jnp.zeros((12, C), F32)], axis=0)
            rows = pltpu.roll(rows, shift, 0)
            rows = jnp.where(half == 0, rows[:, : C // 2], rows[:, C // 2 :])
            first, middle, end = rows[0:16], rows[16:32], rows[32:48]
            shards_in[conv, ha, core, half, column, 2 * a] = jnp.where(row_half >= shift, first, end).astype(BF16)
            shards_in[conv, ha, core, half, column, 2 * a + 1] = middle.astype(BF16)
            end = pltpu.roll(end, lax.rem(4 * a - shift + 16, 16), 0)
            spare = end if a == 0 else jnp.where(row_half >= 4 * a, end, spare)
        shards_in[conv, ha, core, half, column, 6] = spare.astype(BF16)

    def weight_copy(ref, sems, spot, device):
        return pltpu.make_async_remote_copy(
            src_ref=ref, dst_ref=ref, send_sem=sems[0].at[spot], recv_sem=sems[1].at[spot],
            device_id=device, device_id_type=MESH,
        )

    def along_ha(conv):
        ref = shards_in.at[conv, ha, core, half, column]
        return [weight_copy(ref, (y_s, y_r), (conv, j), along(1, j)) for j in NEAR]

    def along_wa(conv, j):
        ref = shards_in.at[conv, block(j), core, half, column]
        return [weight_copy(ref, (x_s, x_r), (conv, j), along(2, k)) for k in (2, 6, 4)]

    def along_ta(conv, j):
        ref = shards_in.at[conv, block(j), core, half]
        return [
            weight_copy(ref.at[pl.ds(0, 2)], (z_s, z_r), (conv, j, 0), along(0, 1)),
            weight_copy(ref.at[pl.ds(2, 2)], (z_s, z_r), (conv, j, 1), along(0, N - 1)),
        ]

    def across(conv, j):
        return [weight_copy(shards_in.at[conv, block(j), core], (c_s, c_r), (conv, j), sibling)]

    def start(copies):
        for copy in copies:
            copy.start()

    def arrived(ref, sem):
        pltpu.make_async_copy(ref, ref, sem).wait()

    def weights_out(conv):
        start(along_ha(conv))
        start(along_wa(conv, 0))

    def from_ha(conv, j):
        arrived(shards_in.at[conv, block(j), core, half, 0], y_r.at[conv, j])
        start(along_wa(conv, j))

    def from_wa(conv, j):
        arrived(shards_in.at[conv, block(j), core, half, pl.ds(0, 3)], x_r.at[conv, j])
        start(along_ta(conv, j))

    def from_ta(conv, j):
        ref = shards_in.at[conv, block(j), core, 1 - half]
        arrived(ref.at[pl.ds(0, 2)], z_r.at[conv, j, 0])
        arrived(ref.at[pl.ds(2, 2)], z_r.at[conv, j, 1])
        start(across(conv, j))

    def from_sibling(conv, j):
        arrived(shards_in.at[conv, block(j), 1 - core], c_r.at[conv, j])
        spot = block(j)

        def merge(g, carry):
            for s in range(2):
                def tile(p, i):
                    return shards_in[conv, spot, p % 2, s, 2 * g + p // 2, i].astype(F32)

                spare = [tile(p, 6) for p in range(4)]
                for a in range(3):
                    heads = [tile(p, 2 * a) for p in range(4)]
                    tiles = [heads[0]]
                    for p in range(4):
                        tiles.append(tile(p, 2 * a + 1))
                        end = pltpu.roll(spare[p], (4 * (p - a)) % 16, 0) if p != a else spare[p]
                        if p < 3:
                            end = jnp.where(row_half < 4 * p + 4, end, heads[p + 1])
                        tiles.append(jnp.where(row_half < 4 * p, heads[p], end) if p else end)
                    for i, value in enumerate(tiles):
                        wb[conv, a, 18 * spot + 9 * g + i, :, s * (C // 2) : (s + 1) * (C // 2)] = value.astype(BF16)
            return carry

        lax.fori_loop(0, 2, merge, 0)

    def weights_done(conv):
        copies = along_ha(conv)
        for j in range(N):
            copies += along_wa(conv, j) + along_ta(conv, j) + across(conv, j)
        for copy in copies:
            copy.wait_send()

    row_of = lax.broadcasted_iota(jnp.int32, (16, C), 0)

    top, bottom, left, right = ha > 0, ha < N - 1, wa > 0, wa < N - 1

    def put(lhs, t, h, v, before, after, flip):
        before = jnp.where(row_of == 0, before, pltpu.roll(v, 1, 0))
        after = jnp.where(row_of == 15, after, pltpu.roll(v, 15, 0))
        if flip:
            before, after = after, before
        lhs[t, h, :, 0:C] = before.astype(BF16)
        lhs[t, h, :, C : 2 * C] = v.astype(BF16)
        lhs[t, h, :, 2 * C : 3 * C] = after.astype(BF16)

    def fill_frame(lhs, t, frame, cell, side, corner, flip):
        edges = []
        for r, ok in ((0, left), (1, right)):
            ok = jnp.logical_and(ok, frame)
            mid = jnp.where(ok, side(r), 0.0)
            hi = jnp.where(jnp.logical_and(ok, top), corner(r, 0), 0.0)
            lo = jnp.where(jnp.logical_and(ok, bottom), corner(r, 1), 0.0)
            edges.append([hi] + [mid[h : h + 1] for h in range(8)] + [lo])
        for h in range(10):
            ok = frame
            if h == 0:
                ok = jnp.logical_and(ok, top)
            if h == 9:
                ok = jnp.logical_and(ok, bottom)
            put(lhs, t, h, jnp.where(ok, cell(h), 0.0), edges[0][h], edges[1][h], flip)

    def fill(lhs, refs, early, late, fn, flip):
        def body(t, carry):
            frame = jnp.logical_and(jnp.logical_or(t >= 2, early), jnp.logical_or(t < 2, late))
            fill_frame(
                lhs, t, frame,
                lambda h: fn(*[x[t, h] for x, _, _ in refs]),
                lambda r: fn(*[k[r, t] for _, k, _ in refs]),
                lambda r, b: fn(*[q[r, b, t] for _, _, q in refs]),
                flip,
            )
            return carry

        lax.fori_loop(0, 4, body, 0)

    def fill_narrow(lhs, field, flip):
        x, k, q, own = fields[field], cols[field], corners[field], OWN[field] // 2
        for t in range(4):
            w, u = t // 2, t % 2
            frame = True if w == own else (ta > 0 if own else ta < N - 1)
            fill_frame(
                lhs, t, frame,
                lambda h: x[t, h].astype(F32),
                lambda r: k[r, w].astype(F32)[8 * u : 8 * u + 8],
                lambda r, b: q[r, b, w].astype(F32)[u : u + 1],
                flip,
            )

    def convolve(lhs, conv, flip):
        total = None
        for a in range(3):
            for b in range(3):
                part = lhs[a : a + 2, b : b + 8].reshape(CELLS, 3 * C)
                if flip:
                    w = wb[conv, 2 - a, pl.ds(48 * (2 - b), 48)].reshape(3 * C, C)
                    out = None
                    for c in range(3):
                        one = lax.dot_general(
                            part[:, c * C : c * C + C], w[c * C : c * C + C, :],
                            (((1,), (1,)), ((), ())), preferred_element_type=F32,
                        )
                        out = one if out is None else out + one
                else:
                    w = wb[conv, a, pl.ds(48 * b, 48)].reshape(3 * C, C)
                    out = jnp.dot(part, w, preferred_element_type=F32)
                total = out if total is None else total + out
        return total.reshape(2, 8, 16, C)

    shard_stage(0, w_one)
    shard_stage(1, w_two)
    load_f.wait()
    moments = local_moments(fx, 2)
    pl.semaphore_wait(barrier, count)
    reduce_send(0, 0, moments)
    weights_out(0)
    halo_send(FEAT)
    reduce_send(0, 1, merge_moments(0, 0))
    from_ha(0, 1)
    from_ha(0, 7)
    from_wa(0, 0)
    from_ha(0, 2)
    from_ha(0, 6)
    from_wa(0, 1)
    reduce_send(0, 2, merge_moments(0, 1))
    from_ha(0, 3)
    from_ha(0, 5)
    from_ha(0, 4)
    from_wa(0, 7)
    from_ta(0, 0)
    from_wa(0, 2)
    weights_out(1)
    from_ta(0, 1)
    centre_1, inv_1 = finish_moments(merge_moments(0, 2))
    g1, b1, g2, b2 = gain_one[...], bias_one[...], gain_two[...], bias_two[...]
    halo_wait(FEAT)

    def act_one(v):
        inner = (v - centre_1) * inv_1 * g1 + b1
        return inner * sigmoid(inner)

    fill(lhs_a, [(fx, fk, fq)], ta > 0, True, act_one, False)
    from_wa(0, 6)
    from_ta(0, 7)
    from_sibling(0, 0)
    from_wa(0, 3)
    from_ta(0, 2)
    from_sibling(0, 1)
    from_wa(0, 5)
    from_ta(0, 6)
    from_sibling(0, 7)
    from_wa(0, 4)
    load_c.wait()
    nx[pl.ds(0, 2), pl.ds(1, 8)] = cx[...].astype(BF16)
    halo_send(COT)
    for j in NEAR:
        from_ha(1, j)
    from_ta(0, 3)
    from_sibling(0, 2)
    from_ta(0, 5)
    from_sibling(0, 6)
    from_ta(0, 4)
    from_sibling(0, 3)
    from_sibling(0, 5)
    from_sibling(0, 4)

    hx[pl.ds(0, 2), pl.ds(1, 8)] = convolve(lhs_a, 0, False)
    reduce_send(1, 0, local_moments(hx, 0))
    for j in (0, 1, 7):
        from_wa(1, j)
    reduce_send(1, 1, merge_moments(1, 0))
    for j, k in ((2, 0), (6, 1), (3, 7)):
        from_wa(1, j)
        from_ta(1, k)
    reduce_send(1, 2, merge_moments(1, 1))
    for j, k, m in ((5, 2, 0), (4, 6, 1)):
        from_wa(1, j)
        from_ta(1, k)
        from_sibling(1, m)
    halo_send(HID)
    for j, k in ((3, 7), (5, 2), (4, 6)):
        from_ta(1, j)
        from_sibling(1, k)
    for j in (3, 5, 4):
        from_sibling(1, j)
    halo_wait(COT)
    fill_narrow(lhs_b, COT, True)
    gx[pl.ds(0, 2), pl.ds(1, 8)] = convolve(lhs_b, 1, True)
    halo_send(GRAD)
    centre_2, inv_2 = finish_moments(merge_moments(1, 2))

    def back_sums(field, own, grad, centre, inv, gain, bias):
        def body(i, carry):
            gain_sum, bias_sum = carry
            t, h = i // 8, i % 8
            unit = (field[own + t, 1 + h] - centre) * inv
            inner = unit * gain + bias
            s = sigmoid(inner)
            gi = grad(t, h) * s * (1.0 + inner * (1.0 - s))
            inner_grad[i] = gi
            unit_buf[i] = unit
            return gain_sum + gi * unit, bias_sum + gi

        zero = jnp.zeros((16, C), F32)
        sums = lax.fori_loop(0, 16, body, (zero, zero))
        return jnp.concatenate([jnp.sum(s, axis=0, keepdims=True) for s in sums], axis=0)

    reduce_send(2, 0, back_sums(hx, 0, lambda t, h: gx[t, 1 + h], centre_2, inv_2, g2, b2))

    def act_two(i, carry):
        inner = unit_buf[i] * g2 + b2
        mx[2 + i // 8, 1 + i % 8] = (inner * sigmoid(inner)).astype(BF16)
        return carry

    lax.fori_loop(0, 16, act_two, 0)
    halo_send(ACT)
    reduce_send(2, 1, merge_sums(2, 0))
    halo_wait(ACT)
    fill_narrow(lhs_a, ACT, False)
    reduce_send(2, 2, merge_sums(2, 1))
    block_out[...] = fx[pl.ds(2, 2), pl.ds(1, 8)] + convolve(lhs_a, 1, False)
    halo_wait(HID)
    halo_wait(GRAD)
    sums_2 = merge_sums(2, 2)
    norm_grads[2:4, :] = sums_2
    members = float(CELLS * N**3 * GROUP)
    both = group_sum(sums_2 * g2) * (1.0 / members)
    first_2, second_2 = both[1:2], both[0:1]

    def grad_hidden(v, g):
        unit = (v - centre_2) * inv_2
        inner = unit * g2 + b2
        s = sigmoid(inner)
        gi = g * s * (1.0 + inner * (1.0 - s))
        return (gi * g2 - first_2 - unit * second_2) * inv_2

    fill(lhs_b, [(hx, hk, hq), (gx, gk, gq)], True, ta < N - 1, grad_hidden, True)
    grad_act = convolve(lhs_b, 0, True)
    ga[...] = grad_act

    reduce_send(3, 0, back_sums(fx, 2, lambda t, h: ga[t, h], centre_1, inv_1, g1, b1))
    for field in (FEAT, COT, HID, ACT):
        halo_done(field)
    reduce_send(3, 1, merge_sums(3, 0))
    for conv in (0, 1):
        weights_done(conv)
    reduce_send(3, 2, merge_sums(3, 1))
    halo_done(GRAD)
    sums_1 = merge_sums(3, 2)
    norm_grads[0:2, :] = sums_1
    both = group_sum(sums_1 * g1) * (1.0 / members)
    first_1, second_1 = both[1:2], both[0:1]

    def last(i, carry):
        t, h = i // 8, i % 8
        field = (inner_grad[i] * g1 - first_1 - unit_buf[i] * second_1) * inv_1
        grad_input[t, h] = cx[t, h] + field
        return carry

    lax.fori_loop(0, 16, last, 0)
    for k in range(4):
        for s in range(3):
            for copy in reduce_copies(k, s):
                copy.wait_send()


def shards(features, cotangent, conv_one, conv_two, gain_one, bias_one, gain_two, bias_two):
    vmem = pl.BlockSpec(memory_space=pltpu.VMEM)
    anywhere = pl.BlockSpec(memory_space=pl.ANY)

    def buf(*shape, dtype=F32):
        return pltpu.VMEM(shape, dtype)

    scratch = (
        [buf(2, 8, 16, C)]
        + [buf(4, 10, 16, C)] * 3
        + [buf(4, 10, 16, C, dtype=BF16)] * 2
        + [buf(2, 4, 8, C)] * 3
        + [buf(2, 2, 16, C, dtype=BF16)] * 2
        + [buf(2, 2, 4, 1, C)] * 3
        + [buf(2, 2, 2, 16, C, dtype=BF16)] * 2
        + [buf(3, 2, 2, 8, C), buf(3, 2, 2, 2, 1, C)]
        + [buf(2, 2, 16, C, dtype=BF16), buf(2, 2, 2, 16, C, dtype=BF16)]
        + [buf(4, 10, 16, 3 * C, dtype=BF16)] * 2
        + [buf(2, N, 2, 2, 4, 7, 16, C // 2, dtype=BF16)]
        + [buf(2, 3, 144, 16, C, dtype=BF16)]
        + [buf(4, 3, 2, C), buf(4, 3, N, 2, C)]
        + [buf(16, 16, C)] * 2
        + [buf(2, 8, 16, C)]
        + [pltpu.SemaphoreType.DMA((2,))]
        + [pltpu.SemaphoreType.DMA((4, 3))] * 2
        + [pltpu.SemaphoreType.DMA((5, 27))] * 2
        + [pltpu.SemaphoreType.DMA((2, N))] * 4
        + [pltpu.SemaphoreType.DMA((2, N, 2))] * 2
        + [pltpu.SemaphoreType.DMA((2, N))] * 2
    )
    block = jax.ShapeDtypeStruct((2, 8, 16, C), F32)
    return pl.pallas_call(
        kernel,
        out_shape=(block, block, jax.ShapeDtypeStruct((4, C), F32)),
        in_specs=[anywhere] * 2 + [vmem] * 6,
        out_specs=(vmem, vmem, vmem),
        scratch_shapes=scratch,
        compiler_params=pltpu.CompilerParams(
            collective_id=0, has_side_effects=True, vmem_limit_bytes=56 * 2**20
        ),
    )(
        features, cotangent, conv_one, conv_two,
        gain_one[None], bias_one[None], gain_two[None], bias_two[None],
    )


def solution(mesh):
    return jax.shard_map(
        shards,
        mesh=mesh,
        in_specs=(
            P("ta", "ha", "wa", None),
            P("ta", "ha", "wa", None),
            P(None, ("ha", "wa"), None),
            P(None, ("ha", "wa"), None),
            P(),
            P(),
            P(),
            P(),
        ),
        out_specs=(P("ta", "ha", "wa", None), P("ta", "ha", "wa", None), P()),
        check_vma=False,
    )
```

time: 117 us -> 98.6 us (0.84)
  Pallas kernels: 113 us -> 94.5 us
    pallas_call x1, Pallas kernels: 113 us -> 94.5 us  [shards(): pl.pallas_call(kernel, out_shape=(block, block, jax.ShapeDtypeStruct((4,...]
where the time goes in v2:
time: 98.6 us; the launch traced here: 98.1 us
  Pallas kernels  94.5 us (96%)
  local copies, waits for them, and re-layouts  3.02 us (3%)
    pallas_call x1, Pallas kernels, shards(): pl.pallas_call(kernel, out_shape=(block, block, jax.ShapeDtypeStruct((4,...  94.5 us
    unnamed x7, local copies, waits for them, and re-layouts  3.02 us

profile of v2, /device:TPU:1, one launch (start us, length us, event | category | flops | bytes accessed | tf_op | source)
XLA Modules:
  0.0 98.1 jit_solution(584994932048397699)
XLA Ops:
  0.6 94.5 %shard_map.103 = (f32[2,8,16,256]{3,2,1,0:T(8,128)}, f32[2,8,16,256]{3,2,1,0:T(8,128)}, f32[4,256]{1,0:T(4,128)}) custom-call(f32[2,8,16,256]{3,2,1,0:T(8,128)} %feat.1, f32[2,8,16,256]{3,2,1,0:T(8,128)} %cot.1, bf16[3,36,256]{2,1,0:T(8,128)(2,1)} %w_one.1, bf16[3,36,256]{2,1,0:T(8,128)(2,1)} %w_two.1, f32[1,256]{1,0:T(1,128)} %bitcast.4, f32[1,256]{1,0:T(1,128)} %bitcast.5, ...), custom_call_target="tpu_custom_call" | custom-call | tf_op jit(solution)/shard_map/pallas_call | solution.py:562
  95.1 0.0 copy-start
  95.1 1.7 %copy.14 = f32[2,8,16,256]{3,2,1,0:T(8,128)} copy(f32[2,8,16,256]{3,2,1,0:T(8,128)} %get-tuple-element.6) | data formatting | bytes 524288
  96.8 0.0 copy-done
  96.8 0.0 copy-start.1
  96.8 0.7 copy.15
  97.6 0.0 copy-done.1
  97.6 0.6 copy.16
Async XLA Ops:
  95.1 1.7 %copy-start = (f32[2,8,16,256]{3,2,1,0:T(8,128)S(1)}, f32[2,8,16,256]{3,2,1,0:T(8,128)}, u32[]{:S(2)}) copy-start(f32[2,8,16,256]{3,2,1,0:T(8,128)} %get-tuple-element.7) | copy-start | bytes 786436
  96.8 0.7 copy-start.1

commit v3 on v2

--- a/solution.py
+++ b/solution.py
@@ -12,6 +12,7 @@
 C = 256
 GROUP = 8
 NEAR = (1, 7, 2, 6, 3, 5, 4)
+ORDER = ((0, 2, 1), (2, 1, 0), (2, 1, 0), (2, 1, 0))
 EPS = 1e-06
 CELLS = 256
 MESH = pl.DeviceIdType.MESH
@@ -76,7 +77,7 @@
     load_c.start()
 
     def reduce_copies(k, s):
-        axis = 2 - s
+        axis = ORDER[k][s]
         return [
             pltpu.make_async_remote_copy(
                 src_ref=stage.at[k, s],
@@ -91,7 +92,7 @@
 
     def reduce_send(k, s, value):
         stage[k, s] = value
-        board[k, s, me[2 - s]] = value
+        board[k, s, me[ORDER[k][s]]] = value
         for copy in reduce_copies(k, s):
             copy.start()
 
@@ -245,10 +246,6 @@
     def arrived(ref, sem):
         pltpu.make_async_copy(ref, ref, sem).wait()
 
-    def weights_out(conv):
-        start(along_ha(conv))
-        start(along_wa(conv, 0))
-
     def from_ha(conv, j):
         arrived(shards_in.at[conv, block(j), core, half, 0], y_r.at[conv, j])
         start(along_wa(conv, j))
@@ -377,24 +374,34 @@
     moments = local_moments(fx, 2)
     pl.semaphore_wait(barrier, count)
     reduce_send(0, 0, moments)
-    weights_out(0)
+    start(along_ha(0))
+    start(along_wa(0, 0))
     halo_send(FEAT)
-    reduce_send(0, 1, merge_moments(0, 0))
+    start(along_ha(1))
     from_ha(0, 1)
     from_ha(0, 7)
     from_wa(0, 0)
     from_ha(0, 2)
     from_ha(0, 6)
+    reduce_send(0, 1, merge_moments(0, 0))
     from_wa(0, 1)
-    reduce_send(0, 2, merge_moments(0, 1))
     from_ha(0, 3)
     from_ha(0, 5)
+    from_wa(0, 7)
     from_ha(0, 4)
-    from_wa(0, 7)
+    start(along_wa(1, 0))
+    from_ha(1, 1)
     from_ta(0, 0)
     from_wa(0, 2)
-    weights_out(1)
-    from_ta(0, 1)
+    reduce_send(0, 2, merge_moments(0, 1))
+    for j, k, m in ((1, 6, 7), (7, 3, 2), (2, 5, 6), (6, 4, 3)):
+        from_ta(0, j)
+        from_wa(0, k)
+        from_ha(1, m)
+    from_ha(1, 5)
+    from_ha(1, 4)
+    load_c.wait()
+    nx[pl.ds(0, 2), pl.ds(1, 8)] = cx[...].astype(BF16)
     centre_1, inv_1 = finish_moments(merge_moments(0, 2))
     g1, b1, g2, b2 = gain_one[...], bias_one[...], gain_two[...], bias_two[...]
     halo_wait(FEAT)
@@ -404,48 +411,35 @@
         return inner * sigmoid(inner)
 
     fill(lhs_a, [(fx, fk, fq)], ta > 0, True, act_one, False)
-    from_wa(0, 6)
-    from_ta(0, 7)
-    from_sibling(0, 0)
-    from_wa(0, 3)
-    from_ta(0, 2)
-    from_sibling(0, 1)
-    from_wa(0, 5)
-    from_ta(0, 6)
-    from_sibling(0, 7)
-    from_wa(0, 4)
-    load_c.wait()
-    nx[pl.ds(0, 2), pl.ds(1, 8)] = cx[...].astype(BF16)
     halo_send(COT)
-    for j in NEAR:
-        from_ha(1, j)
+    for j in (0, 1, 7, 2):
+        from_sibling(0, j)
     from_ta(0, 3)
-    from_sibling(0, 2)
+    from_wa(1, 0)
     from_ta(0, 5)
     from_sibling(0, 6)
     from_ta(0, 4)
+    from_wa(1, 1)
     from_sibling(0, 3)
+    from_wa(1, 7)
     from_sibling(0, 5)
     from_sibling(0, 4)
 
     hx[pl.ds(0, 2), pl.ds(1, 8)] = convolve(lhs_a, 0, False)
     reduce_send(1, 0, local_moments(hx, 0))
-    for j in (0, 1, 7):
-        from_wa(1, j)
-    reduce_send(1, 1, merge_moments(1, 0))
     for j, k in ((2, 0), (6, 1), (3, 7)):
         from_wa(1, j)
         from_ta(1, k)
-    reduce_send(1, 2, merge_moments(1, 1))
-    for j, k, m in ((5, 2, 0), (4, 6, 1)):
+    reduce_send(1, 1, merge_moments(1, 0))
+    for j, k in ((5, 2), (4, 6)):
         from_wa(1, j)
         from_ta(1, k)
-        from_sibling(1, m)
-    halo_send(HID)
-    for j, k in ((3, 7), (5, 2), (4, 6)):
+    for j, k in ((3, 0), (5, 1), (4, 7)):
         from_ta(1, j)
         from_sibling(1, k)
-    for j in (3, 5, 4):
+    reduce_send(1, 2, merge_moments(1, 1))
+    halo_send(HID)
+    for j in (2, 6, 3, 5, 4):
         from_sibling(1, j)
     halo_wait(COT)
     fill_narrow(lhs_b, COT, True)
@@ -526,6 +520,15 @@
         for s in range(3):
             for copy in reduce_copies(k, s):
                 copy.wait_send()
+
+
+def write_out(*refs):
+    sems = refs[6]
+    copies = [pltpu.make_async_copy(refs[i], refs[3 + i], sems.at[i]) for i in range(3)]
+    for copy in copies:
+        copy.start()
+    for copy in copies:
+        copy.wait()
 
 
 def shards(features, cotangent, conv_one, conv_two, gain_one, bias_one, gain_two, bias_two):
@@ -558,10 +561,10 @@
         + [pltpu.SemaphoreType.DMA((2, N, 2))] * 2
         + [pltpu.SemaphoreType.DMA((2, N))] * 2
     )
-    block = jax.ShapeDtypeStruct((2, 8, 16, C), F32)
-    return pl.pallas_call(
+    sizes = ((2, 8, 16, C), (2, 8, 16, C), (4, C))
+    results = pl.pallas_call(
         kernel,
-        out_shape=(block, block, jax.ShapeDtypeStruct((4, C), F32)),
+        out_shape=tuple(pltpu.VMEM(size, F32) for size in sizes),
         in_specs=[anywhere] * 2 + [vmem] * 6,
         out_specs=(vmem, vmem, vmem),
         scratch_shapes=scratch,
@@ -572,6 +575,13 @@
         features, cotangent, conv_one, conv_two,
         gain_one[None], bias_one[None], gain_two[None], bias_two[None],
     )
+    return pl.pallas_call(
+        write_out,
+        out_shape=tuple(jax.ShapeDtypeStruct(size, F32) for size in sizes),
+        in_specs=[vmem] * 3,
+        out_specs=(anywhere,) * 3,
+        scratch_shapes=[pltpu.SemaphoreType.DMA((3,))],
+    )(*results)
 
 
 def solution(mesh):

time: 98.6 us -> 94.4 us (0.957)
  Pallas kernels: 94.5 us -> 91.6 us
  local copies, waits for them, and re-layouts: 3.02 us -> 1.97 us
    pallas_call x1 -> x2, Pallas kernels: 94.5 us -> 91.6 us  [the longest x1 89.7 us: shards(): pl.pallas_call(kernel, out_shape=tuple((pltpu.VMEM(size, F32) for size in...]
    unnamed x7 -> x6, local copies, waits for them, and re-layouts: 3.02 us -> 1.97 us
where the time goes in v3:
time: 94.4 us; the launch traced here: 94.2 us
  Pallas kernels  91.6 us (97%)
  local copies, waits for them, and re-layouts  1.97 us (2%)
    pallas_call x1, Pallas kernels, shards(): pl.pallas_call(kernel, out_shape=tuple((pltpu.VMEM(size, F32) for size in...  89.7 us
    unnamed x6, local copies, waits for them, and re-layouts  1.97 us

profile of v3, /device:TPU:1, one launch (start us, length us, event | category | flops | bytes accessed | tf_op | source)
XLA Modules:
  0.0 94.2 jit_solution(16033182489929297137)
XLA Ops:
  0.6 89.7 %shard_map.103 = (f32[2,8,16,256]{3,2,1,0:T(8,128)S(1)}, f32[2,8,16,256]{3,2,1,0:T(8,128)S(1)}, f32[4,256]{1,0:T(4,128)S(1)}) custom-call(f32[2,8,16,256]{3,2,1,0:T(8,128)} %feat.1, f32[2,8,16,256]{3,2,1,0:T(8,128)} %cot.1, bf16[3,36,256]{2,1,0:T(8,128)(2,1)} %w_one.1, bf16[3,36,256]{2,1,0:T(8,128)(2,1)} %w_two.1, f32[1,256]{1,0:T(1,128)} %bitcast.4, ...), custom_call_target="tpu_custom_call" | custom-call | tf_op jit(solution)/shard_map/pallas_call | solution.py:565
  90.4 0.0 copy-start
  90.4 0.7 copy-done
  91.1 0.0 copy-start.1
  91.1 0.7 copy-done.1
  91.7 0.0 copy-start.2
  91.7 0.6 copy-done.2
  92.3 1.8 %shard_map.104 = (f32[2,8,16,256]{3,2,1,0:T(8,128)}, f32[2,8,16,256]{3,2,1,0:T(8,128)}, f32[4,256]{1,0:T(4,128)}) custom-call(f32[2,8,16,256]{3,2,1,0:T(8,128)} %copy-done, f32[2,8,16,256]{3,2,1,0:T(8,128)} %copy-done.1, f32[4,256]{1,0:T(4,128)} %copy-done.2), custom_call_target="tpu_custom_call" | custom-call | tf_op jit(solution)/shard_map/pallas_call | solution.py:578
Async XLA Ops:
  90.4 0.7 copy-start
  91.1 0.7 copy-start.1
  91.7 0.6 copy-start.2

commit v4 on v3

--- a/solution.py
+++ b/solution.py
@@ -460,7 +460,7 @@
             return gain_sum + gi * unit, bias_sum + gi
 
         zero = jnp.zeros((16, C), F32)
-        sums = lax.fori_loop(0, 16, body, (zero, zero))
+        sums = lax.fori_loop(0, 16, body, (zero, zero), unroll=8)
         return jnp.concatenate([jnp.sum(s, axis=0, keepdims=True) for s in sums], axis=0)
 
     reduce_send(2, 0, back_sums(hx, 0, lambda t, h: gx[t, 1 + h], centre_2, inv_2, g2, b2))
@@ -470,7 +470,7 @@
         mx[2 + i // 8, 1 + i % 8] = (inner * sigmoid(inner)).astype(BF16)
         return carry
 
-    lax.fori_loop(0, 16, act_two, 0)
+    lax.fori_loop(0, 16, act_two, 0, unroll=4)
     halo_send(ACT)
     reduce_send(2, 1, merge_sums(2, 0))
     halo_wait(ACT)
@@ -515,7 +515,7 @@
         grad_input[t, h] = cx[t, h] + field
         return carry
 
-    lax.fori_loop(0, 16, last, 0)
+    lax.fori_loop(0, 16, last, 0, unroll=8)
     for k in range(4):
         for s in range(3):
             for copy in reduce_copies(k, s):
@@ -581,7 +581,7 @@
         in_specs=[vmem] * 3,
         out_specs=(anywhere,) * 3,
         scratch_shapes=[pltpu.SemaphoreType.DMA((3,))],
-    )(*results)
+    )(*[pltpu.with_memory_space_constraint(r, pltpu.VMEM) for r in results])
 
 
 def solution(mesh):

time: 94.4 us -> 91 us (0.964)
  local copies, waits for them, and re-layouts: 1.97 us -> 0 us
  Pallas kernels: 91.6 us -> 90.1 us
    unnamed x6 -> x0, local copies, waits for them, and re-layouts: 1.97 us -> none
    pallas_call x1, Pallas kernels: 1.84 us -> 0.82 us  [shards(): pl.pallas_call(write_out, out_shape=tuple((jax.ShapeDtypeStruct(size, F32...]
where the time goes in v4:
time: 91 us; the launch traced here: 90.8 us
  Pallas kernels  90.1 us (99%)
    pallas_call x1, Pallas kernels, shards(): pl.pallas_call(kernel, out_shape=tuple((pltpu.VMEM(size, F32) for size in...  89.3 us

profile of v4, /device:TPU:1, one launch (start us, length us, event | category | flops | bytes accessed | tf_op | source)
XLA Modules:
  0.0 90.8 jit_solution(6390011532616009835)
XLA Ops:
  0.6 89.3 %shard_map.103 = (f32[2,8,16,256]{3,2,1,0:T(8,128)S(1)}, f32[2,8,16,256]{3,2,1,0:T(8,128)S(1)}, f32[4,256]{1,0:T(4,128)S(1)}) custom-call(f32[2,8,16,256]{3,2,1,0:T(8,128)} %feat.1, f32[2,8,16,256]{3,2,1,0:T(8,128)} %cot.1, bf16[3,36,256]{2,1,0:T(8,128)(2,1)} %w_one.1, bf16[3,36,256]{2,1,0:T(8,128)(2,1)} %w_two.1, f32[1,256]{1,0:T(1,128)} %bitcast.4, ...), custom_call_target="tpu_custom_call" | custom-call | tf_op jit(solution)/shard_map/pallas_call | solution.py:565
  90.0 0.8 shard_map.104

commit v5 on v4

--- a/solution.py
+++ b/solution.py
@@ -12,7 +12,7 @@
 C = 256
 GROUP = 8
 NEAR = (1, 7, 2, 6, 3, 5, 4)
-ORDER = ((0, 2, 1), (2, 1, 0), (2, 1, 0), (2, 1, 0))
+ORDER = ((0, 2, 1), (1, 2, 0), (1, 2, 0), (2, 1, 0))
 EPS = 1e-06
 CELLS = 256
 MESH = pl.DeviceIdType.MESH
@@ -369,15 +369,17 @@
         return total.reshape(2, 8, 16, C)
 
     shard_stage(0, w_one)
-    shard_stage(1, w_two)
-    load_f.wait()
-    moments = local_moments(fx, 2)
     pl.semaphore_wait(barrier, count)
-    reduce_send(0, 0, moments)
     start(along_ha(0))
     start(along_wa(0, 0))
+    load_f.wait()
+    reduce_send(0, 0, local_moments(fx, 2))
     halo_send(FEAT)
+    shard_stage(1, w_two)
     start(along_ha(1))
+    load_c.wait()
+    nx[pl.ds(0, 2), pl.ds(1, 8)] = cx[...].astype(BF16)
+    halo_send(COT)
     from_ha(0, 1)
     from_ha(0, 7)
     from_wa(0, 0)
@@ -400,8 +402,6 @@
         from_ha(1, m)
     from_ha(1, 5)
     from_ha(1, 4)
-    load_c.wait()
-    nx[pl.ds(0, 2), pl.ds(1, 8)] = cx[...].astype(BF16)
     centre_1, inv_1 = finish_moments(merge_moments(0, 2))
     g1, b1, g2, b2 = gain_one[...], bias_one[...], gain_two[...], bias_two[...]
     halo_wait(FEAT)
@@ -411,7 +411,6 @@
         return inner * sigmoid(inner)
 
     fill(lhs_a, [(fx, fk, fq)], ta > 0, True, act_one, False)
-    halo_send(COT)
     for j in (0, 1, 7, 2):
         from_sibling(0, j)
     from_ta(0, 3)

time: 91 us -> 89.9 us (0.988)
  Pallas kernels: 90.1 us -> 89.1 us
    pallas_call x1, Pallas kernels: 89.3 us -> 88.2 us  [shards(): pl.pallas_call(kernel, out_shape=tuple((pltpu.VMEM(size, F32) for size in...]
where the time goes in v5:
time: 89.9 us; the launch traced here: 89.7 us
  Pallas kernels  89.1 us (99%)
    pallas_call x1, Pallas kernels, shards(): pl.pallas_call(kernel, out_shape=tuple((pltpu.VMEM(size, F32) for size in...  88.2 us

profile of v5, /device:TPU:1, one launch (start us, length us, event | category | flops | bytes accessed | tf_op | source)
XLA Modules:
  0.0 89.7 jit_solution(5758879892347088890)
XLA Ops:
  0.6 88.2 %shard_map.103 = (f32[2,8,16,256]{3,2,1,0:T(8,128)S(1)}, f32[2,8,16,256]{3,2,1,0:T(8,128)S(1)}, f32[4,256]{1,0:T(4,128)S(1)}) custom-call(f32[2,8,16,256]{3,2,1,0:T(8,128)} %feat.1, f32[2,8,16,256]{3,2,1,0:T(8,128)} %cot.1, bf16[3,36,256]{2,1,0:T(8,128)(2,1)} %w_one.1, bf16[3,36,256]{2,1,0:T(8,128)(2,1)} %w_two.1, f32[1,256]{1,0:T(1,128)} %bitcast.4, ...), custom_call_target="tpu_custom_call" | custom-call | tf_op jit(solution)/shard_map/pallas_call | solution.py:564
  88.9 0.8 shard_map.104

commit v6 on v5

--- a/solution.py
+++ b/solution.py
@@ -478,31 +478,47 @@
     block_out[...] = fx[pl.ds(2, 2), pl.ds(1, 8)] + convolve(lhs_a, 1, False)
     halo_wait(HID)
     halo_wait(GRAD)
+    halo_done(HID)
+    halo_done(GRAD)
+
+    def scaled(h_ref, g_ref, spot):
+        unit = (h_ref[spot] - centre_2) * inv_2
+        inner = unit * g2 + b2
+        s = sigmoid(inner)
+        gi = g_ref[spot] * s * (1.0 + inner * (1.0 - s))
+        h_ref[spot] = unit * inv_2
+        g_ref[spot] = gi * g2 * inv_2
+
+    def scale_frame(t, carry):
+        for h in range(10):
+            scaled(hx, gx, (t, h))
+        for r in range(2):
+            scaled(hk, gk, (r, t))
+            for b in range(2):
+                scaled(hq, gq, (r, b, t))
+        return carry
+
+    lax.fori_loop(0, 4, scale_frame, 0)
     sums_2 = merge_sums(2, 2)
     norm_grads[2:4, :] = sums_2
     members = float(CELLS * N**3 * GROUP)
     both = group_sum(sums_2 * g2) * (1.0 / members)
     first_2, second_2 = both[1:2], both[0:1]
 
-    def grad_hidden(v, g):
-        unit = (v - centre_2) * inv_2
-        inner = unit * g2 + b2
-        s = sigmoid(inner)
-        gi = g * s * (1.0 + inner * (1.0 - s))
-        return (gi * g2 - first_2 - unit * second_2) * inv_2
+    def grad_hidden(u, g):
+        return g - first_2 * inv_2 - u * second_2
 
     fill(lhs_b, [(hx, hk, hq), (gx, gk, gq)], True, ta < N - 1, grad_hidden, True)
     grad_act = convolve(lhs_b, 0, True)
     ga[...] = grad_act
 
     reduce_send(3, 0, back_sums(fx, 2, lambda t, h: ga[t, h], centre_1, inv_1, g1, b1))
-    for field in (FEAT, COT, HID, ACT):
+    for field in (FEAT, COT, ACT):
         halo_done(field)
     reduce_send(3, 1, merge_sums(3, 0))
     for conv in (0, 1):
         weights_done(conv)
     reduce_send(3, 2, merge_sums(3, 1))
-    halo_done(GRAD)
     sums_1 = merge_sums(3, 2)
     norm_grads[0:2, :] = sums_1
     both = group_sum(sums_1 * g1) * (1.0 / members)

time: 89.9 us -> 89.4 us (level)
  no operation moved by 1% of the time
where the time goes in v6:
time: 89.4 us; the launch traced here: 89.3 us
  Pallas kernels  88.6 us (99%)
    pallas_call x1, Pallas kernels, shards(): pl.pallas_call(kernel, out_shape=tuple((pltpu.VMEM(size, F32) for size in...  87.8 us

profile of v6, /device:TPU:1, one launch (start us, length us, event | category | flops | bytes accessed | tf_op | source)
XLA Modules:
  0.0 89.3 jit_solution(397779603966487025)
XLA Ops:
  0.6 87.8 %shard_map.103 = (f32[2,8,16,256]{3,2,1,0:T(8,128)S(1)}, f32[2,8,16,256]{3,2,1,0:T(8,128)S(1)}, f32[4,256]{1,0:T(4,128)S(1)}) custom-call(f32[2,8,16,256]{3,2,1,0:T(8,128)} %feat.1, f32[2,8,16,256]{3,2,1,0:T(8,128)} %cot.1, bf16[3,36,256]{2,1,0:T(8,128)(2,1)} %w_one.1, bf16[3,36,256]{2,1,0:T(8,128)(2,1)} %w_two.1, f32[1,256]{1,0:T(1,128)} %bitcast.4, ...), custom_call_target="tpu_custom_call" | custom-call | tf_op jit(solution)/shard_map/pallas_call | solution.py:580
  88.4 0.8 shard_map.104
